TPU v7x, 32 devices: a whole 2x2x4 slice. The times are simulated.
32 devices in a mesh: dp: 16 (over z, y, core), seq: 2 (over x).
Axes of the slice: x: 2, y: 2, z: 4, core: 2. Of those that a mesh axis runs over, the one named last changes fastest.
Arguments:
- qkv: bfloat16 [32, 128, 9216], P('dp', 'seq')
- qkv_tan: bfloat16 [32, 128, 9216], P('dp', 'seq'), may hold values from -6 to 6
- positions: int32 [3, 32, 128], P(None, 'dp', 'seq'), may hold values from 0 to 51, as said below
- step_index: int32 [32], P('dp'), may hold values from 0 to 999
- resid: bfloat16 [32, 128, 2560], P('dp', 'seq'), may hold values from -6 to 6
- resid_tan: bfloat16 [32, 128, 2560], P('dp', 'seq'), may hold values from -6 to 6
- noisy: bfloat16 [32, 128, 2560], P('dp', 'seq'), may hold values from -6 to 6
- noisy_tan: bfloat16 [32, 128, 2560], P('dp', 'seq')
- out_weight: bfloat16 [3072, 2560], P(('seq', 'dp')), may hold values from -0.109375 to 0.109375
- gate_bias: float32 [2560], replicated, may hold values from 0.5 to 1.5
- gate_amp: float32 [2560], replicated, may hold values from 0.2 to 0.8
- gate_freq: float32 [2560], replicated, may hold values from 1 to 6
Outputs:
- d_qkv: bfloat16 [32, 128, 9216], P('dp', 'seq')
- d_weight: float32 [3072, 2560], P(('seq', 'dp'))
Inputs may be any that keep to these rules, and one draw needn't show every extreme that they name: positions[0], positions[1], positions[2] are the frame (below 21), row (below 30) and column (below 52) of a token of a latent video grid; the 128 tokens of a clip are consecutive in frame-major order.
All inputs are finite; a program needn't handle non-finite values.
Results may differ from a plain program's by a relative error of at most 0.014.
The roundings to bfloat16 on the way count: a program that leaves them out, or rounds other values in their place, can miss the bound.
Values may be sent and summed in bfloat16 or wider, within the bound.
A program may use at most 128 MiB of HBM per device.

v0:
```python
import math

import jax
import jax.numpy as jnp
from jax import lax
from jax.experimental import pallas as pl
from jax.experimental.pallas import tpu as pltpu
from jax.sharding import PartitionSpec as P

HEAD_DIM = 128
NT = 1000
GRID_H = 30
GRID_W = 52
MESH = pl.DeviceIdType.MESH
PLANES, COLUMNS, CORES = 4, 2, 2


def rope_angles(place):
    pairs = HEAD_DIM // 2
    side = pairs // 3
    first = pairs - 2 * side
    index = jnp.arange(pairs, dtype=jnp.int32)
    part = jnp.where(index < first, 0, jnp.where(index < first + side, 1, 2))
    local = index - jnp.where(part == 0, 0, jnp.where(part == 1, first, first + side))
    count = jnp.where(part == 0, first, side)
    freq = jnp.exp(-math.log(10000.0) * local.astype(jnp.float32) / count.astype(jnp.float32))
    spot = place.astype(jnp.float32)
    chosen = jnp.where(
        part == 0, spot[0][..., None], jnp.where(part == 1, spot[1][..., None], spot[2][..., None])
    )
    return chosen * freq


def rotate(values, cosine, sine, sign):
    pairs = values.shape[-1] // 2
    first = values[..., :pairs]
    second = values[..., pairs:]
    return jnp.concatenate(
        [first * cosine - sign * second * sine, sign * first * sine + second * cosine], -1
    )


def body(
    qkv,
    qkv_tan,
    positions,
    step_index,
    resid,
    resid_tan,
    noisy,
    noisy_tan,
    out_weight,
    gate_bias,
    gate_amp,
    gate_freq,
):
    f32 = jnp.float32
    brain_float_half = jnp.bfloat16
    clips, len_dev, triple = qkv.shape
    att = triple // 3
    heads = att // HEAD_DIM
    groups = lax.axis_size("seq")
    heads_dev = heads // groups
    att_dev = att // groups
    seq_len = len_dev * groups
    width = resid.shape[2]
    token_count = lax.axis_size("dp") * clips * seq_len
    logit_scale = 1.0 / math.sqrt(HEAD_DIM)
    angle = rope_angles(positions)
    cosine = jnp.cos(angle)[:, :, None, None, :]
    sine = jnp.sin(angle)[:, :, None, None, :]

    def prepare(block):
        parts = block.reshape(clips, len_dev, 3, heads, HEAD_DIM)
        turned = rotate(parts[:, :, :2].astype(f32), cosine, sine, 1.0).astype(brain_float_half)
        return jnp.concatenate([turned, parts[:, :, 2:]], 2).reshape(clips, len_dev, 3, att)

    mixed, mixed_tan = (
        lax.all_to_all(prepare(qkv), "seq", split_axis=3, concat_axis=1, tiled=True),
        lax.all_to_all(prepare(qkv_tan), "seq", split_axis=3, concat_axis=1, tiled=True),
    )

    def split_heads(block, slot):
        return block[:, :, slot].reshape(clips, seq_len, heads_dev, HEAD_DIM)

    query_rows = split_heads(mixed, 0)
    key_rows = split_heads(mixed, 1)
    value_rows = split_heads(mixed, 2)
    query_tangent = split_heads(mixed_tan, 0)
    key_tangent = split_heads(mixed_tan, 1)
    value_tangent = split_heads(mixed_tan, 2)
    score_matrix = (
        jnp.einsum("clhd,cmhd->chlm", query_rows, key_rows, preferred_element_type=f32)
        * logit_scale
    )
    probs = jax.nn.softmax(score_matrix, axis=-1)
    low_precision_probs = probs.astype(brain_float_half)
    attention_output = jnp.einsum(
        "chlm,cmhd->lchd", low_precision_probs, value_rows, preferred_element_type=f32
    ).astype(brain_float_half)
    score_tangent = (
        jnp.einsum(
            "clhe,cmhe->chlm",
            jnp.concatenate([query_tangent, query_rows], -1),
            jnp.concatenate([key_rows, key_tangent], -1),
            preferred_element_type=f32,
        )
        * logit_scale
    )
    dprob = probs * (score_tangent - jnp.sum(probs * score_tangent, axis=-1, keepdims=True))
    prob_tangent_grad = dprob.astype(brain_float_half)
    attention_output_tangent = jnp.einsum(
        "chlm,cmhd->lchd",
        jnp.concatenate([prob_tangent_grad, low_precision_probs], -1),
        jnp.concatenate([value_rows, value_tangent], 1),
        preferred_element_type=f32,
    ).astype(brain_float_half)
    flat = attention_output.reshape(seq_len, clips, att_dev)
    rows = jnp.stack([attention_output, attention_output_tangent], 1).reshape(
        seq_len, 2, clips, att_dev
    )
    part = rows
    partial_value = jnp.einsum(
        "lsck,kd->lscd",
        part,
        lax.all_gather(out_weight, "dp", axis=0, tiled=True),
        preferred_element_type=f32,
    )
    sums = lax.psum_scatter(
        partial_value.astype(jnp.bfloat16), "seq", scatter_dimension=0, tiled=True
    ).astype(jnp.float32)
    proj = jnp.moveaxis(sums[:, 0], 0, 1)
    proj_tan = jnp.moveaxis(sums[:, 1], 0, 1)
    time = 0.05 + 1.47 * (step_index.astype(f32) + 0.5) / NT
    phase = gate_freq[None, None, :] * time[:, None, None]
    gate = gate_bias + gate_amp * jnp.sin(phase)
    slope = gate_amp * gate_freq * jnp.cos(phase)
    out = resid.astype(f32) + gate * proj
    out_tan = resid_tan.astype(f32) + gate * proj_tan + slope * proj
    cos_sq = (jnp.cos(time) ** 2)[:, None, None]
    cross = (jnp.cos(time) * jnp.sin(time))[:, None, None]
    target = -cos_sq * (0.5 * out - noisy_tan.astype(f32)) - cross * (
        noisy.astype(f32) + 0.5 * out_tan
    )
    local_sq = jnp.sum(target * target, axis=(1, 2))
    total_sq = lax.psum(local_sq, "seq")
    rms = jnp.sqrt(total_sq / (seq_len * width) + 1e-06)[:, None, None]
    cot = -2.0 * target / (rms + 0.1)
    grad_proj = (gate * cot).astype(brain_float_half)
    grad_all = lax.all_gather(grad_proj, "seq", axis=1, tiled=True)
    attention_gradient = jnp.einsum(
        "fev,hv->feh",
        grad_all,
        lax.all_gather(out_weight, "dp", axis=0, tiled=True),
        preferred_element_type=f32,
    ).astype(brain_float_half)
    part = flat
    d_weight = lax.psum_scatter(
        jnp.einsum("lck,cld->kd", part, grad_all, preferred_element_type=f32).astype(jnp.bfloat16),
        "dp",
        scatter_dimension=0,
        tiled=True,
    ).astype(jnp.float32) / math.sqrt(token_count)
    attention_gradient = attention_gradient.reshape(clips, seq_len, heads_dev, HEAD_DIM)
    value_gradient = jnp.einsum(
        "chlm,clhd->cmhd", low_precision_probs, attention_gradient, preferred_element_type=f32
    ).astype(brain_float_half)
    probability_gradient = jnp.einsum(
        "clhd,cmhd->chlm", attention_gradient, value_rows, preferred_element_type=f32
    )
    score_gradient = (
        probs
        * (probability_gradient - jnp.sum(probs * probability_gradient, axis=-1, keepdims=True))
        * logit_scale
    ).astype(brain_float_half)
    query_gradient = jnp.einsum(
        "chlm,cmhd->clhd", score_gradient, key_rows, preferred_element_type=f32
    ).astype(brain_float_half)
    key_gradient = jnp.einsum(
        "chlm,clhd->cmhd", score_gradient, query_rows, preferred_element_type=f32
    ).astype(brain_float_half)
    stacked = jnp.stack([query_gradient, key_gradient, value_gradient], 2).reshape(
        clips, seq_len, 3, att_dev
    )
    back = lax.all_to_all(stacked, "seq", split_axis=1, concat_axis=3, tiled=True)
    parts = back.reshape(clips, len_dev, 3, heads, HEAD_DIM)
    turned = rotate(parts[:, :, :2].astype(f32), cosine, sine, -1.0).astype(brain_float_half)
    d_qkv = jnp.concatenate([turned, parts[:, :, 2:]], 2).reshape(clips, len_dev, 3 * att)
    return (d_qkv, d_weight)


def multiple(value, of):
    return pl.multiple_of(value, of)


def dot(left, right, left_dim, right_dim):
    return lax.dot_general(
        left, right, (((left_dim,), (right_dim,)), ((), ())), preferred_element_type=jnp.float32
    )


def softmax_rows(scores):
    shifted = jnp.exp(scores - jnp.max(scores, axis=-1, keepdims=True))
    return shifted / jnp.sum(shifted, axis=-1, keepdims=True)


def turn(block, cosine, sine):
    wide = block.astype(jnp.float32)
    return (wide * cosine + pltpu.roll(wide, HEAD_DIM // 2, 1) * sine).astype(jnp.bfloat16)


def forward_kernel(
    qkv, qkv_tan, angle, rows, turned, cos_out, sin_out, arrived, send_sem, recv_sem, own_sem
):
    me = lax.axis_index("seq")
    other = 1 - me
    clips, len_dev, triple = qkv.shape
    att = triple // 3
    att_dev = att // 2
    chunks = send_sem.shape[1]
    chunk = att_dev // chunks
    scale = 1.0 / math.sqrt(HEAD_DIM)

    barrier = pltpu.get_barrier_semaphore()
    pl.semaphore_signal(barrier, inc=1, device_id={"seq": other}, device_id_type=MESH)
    pl.semaphore_wait(barrier, 1)

    def copies(clip, part):
        result = []
        for which, source in enumerate((qkv, qkv_tan)):
            for slot in range(3):
                place = arrived.at[
                    clip,
                    which * 3 + slot,
                    pl.ds(multiple(me * len_dev, 64), len_dev),
                    pl.ds(multiple(part * chunk, 128), chunk),
                ]
                theirs = multiple(slot * att + other * att_dev + part * chunk, 128)
                mine = multiple(slot * att + me * att_dev + part * chunk, 128)
                result.append(
                    (
                        pltpu.make_async_remote_copy(
                            src_ref=source.at[clip, :, pl.ds(theirs, chunk)],
                            dst_ref=place,
                            send_sem=send_sem.at[clip, part, which * 3 + slot],
                            recv_sem=recv_sem.at[clip, part, which * 3 + slot],
                            device_id={"seq": other},
                            device_id_type=MESH,
                        ),
                        pltpu.make_async_copy(
                            source.at[clip, :, pl.ds(mine, chunk)],
                            place,
                            own_sem.at[clip, part, which * 3 + slot],
                        ),
                    )
                )
        return result

    def start(step, carry):
        for remote, own in copies(step // chunks, step % chunks):
            remote.start()
            own.start()
        return carry

    lax.fori_loop(0, clips * chunks, start, 0)
    lane = lax.broadcasted_iota(jnp.int32, angle.shape, 2)
    sines = jnp.sin(angle[...])
    cos_out[...] = jnp.cos(angle[...])
    sin_out[...] = jnp.where(lane < HEAD_DIM // 2, -sines, sines)

    def attend(step, carry):
        clip, part = step // chunks, step % chunks
        for remote, own in copies(clip, part):
            remote.wait()
            own.wait()
        cosine, sine = cos_out[clip], sin_out[clip]
        for head in range(chunk // HEAD_DIM):
            at = pl.ds(multiple(part * chunk + head * HEAD_DIM, 128), HEAD_DIM)
            query = turn(arrived[clip, 0, :, at], cosine, sine)
            key = turn(arrived[clip, 1, :, at], cosine, sine)
            value = arrived[clip, 2, :, at]
            query_tan = turn(arrived[clip, 3, :, at], cosine, sine)
            key_tan = turn(arrived[clip, 4, :, at], cosine, sine)
            value_tan = arrived[clip, 5, :, at]
            turned[clip, 0, :, at] = query
            turned[clip, 1, :, at] = key
            turned[clip, 2, :, at] = value
            probs = softmax_rows(dot(query, key, 1, 1) * scale)
            low = probs.astype(jnp.bfloat16)
            length = low.shape[0]
            rows[clip, :length, at] = dot(low, value, 1, 0).astype(jnp.bfloat16)
            dscore = scale * dot(
                jnp.concatenate([query_tan, query], 1), jnp.concatenate([key, key_tan], 1), 1, 1
            )
            dprob = probs * (dscore - jnp.sum(probs * dscore, axis=-1, keepdims=True))
            both = jnp.concatenate([dprob.astype(jnp.bfloat16), low], 1)
            rows[clip, length:, at] = dot(
                both, jnp.concatenate([value, value_tan], 0), 1, 0
            ).astype(jnp.bfloat16)
        return carry

    lax.fori_loop(0, clips * chunks, attend, 0)


def backward_kernel(
    weight,
    rows,
    turned,
    known,
    coef,
    cos_tab,
    sin_tab,
    d_qkv,
    d_weight,
    total,
    outgoing,
    incoming,
    grad_proj,
    grads,
    partial,
    from_core,
    from_column,
    from_plane,
    swap_send,
    swap_recv,
    grad_send,
    grad_recv,
    grad_own,
    core_send,
    core_recv,
    column_send,
    column_recv,
    plane_send,
    plane_recv,
):
    f32, half = jnp.float32, jnp.bfloat16
    me = lax.axis_index("seq")
    other = 1 - me
    place = lax.axis_index("dp")
    plane, column, core = place // (COLUMNS * CORES), (place // CORES) % COLUMNS, place % CORES

    def index(at_plane, at_column, at_core):
        return (at_plane * COLUMNS + at_column) * CORES + at_core

    clips, length, width = total.shape
    att_dev = weight.shape[0]
    len_dev = length // 2
    att = att_dev * 2
    scale = 1.0 / math.sqrt(HEAD_DIM)
    block = d_weight.shape[0]
    tiles = swap_send.shape[1]
    tile = width // tiles
    chunks = grad_send.shape[1]
    chunk = att_dev // chunks
    token_count = lax.axis_size("dp") * clips * length

    barrier = pltpu.get_barrier_semaphore()
    pl.semaphore_signal(barrier, inc=1, device_id={"seq": other}, device_id_type=MESH)
    partners = [index(plane, column, 1 - core), index(plane, 1 - column, core)]
    partners += [index((plane + 1 + step) % PLANES, column, core) for step in range(PLANES - 1)]
    for partner in partners:
        pl.semaphore_signal(barrier, inc=1, device_id={"dp": partner}, device_id_type=MESH)
    pl.semaphore_wait(barrier, 1 + len(partners))

    def swap(clip, part):
        at = pl.ds(multiple(part * tile, 128), tile)
        return pltpu.make_async_remote_copy(
            src_ref=outgoing.at[clip, :, at],
            dst_ref=incoming.at[clip, :, at],
            send_sem=swap_send.at[clip, part],
            recv_sem=swap_recv.at[clip, part],
            device_id={"seq": other},
            device_id_type=MESH,
        )

    def project(step, carry):
        clip, part = step // tiles, step % tiles
        at = pl.ds(multiple(part * tile, 128), tile)
        both = dot(rows[clip], weight[:, at], 1, 0).astype(half).astype(f32)
        total[clip, :, at] = (
            coef[clip, 0:1, at] * both[:length] + coef[clip, 1:2, at] * both[length:]
        )
        mine = pl.ds(multiple(me * len_dev, 64), len_dev)
        total[clip, mine, at] = total[clip, mine, at] + known[clip, :, at]
        outgoing[clip, :, at] = total[clip, :, at].astype(half)
        swap(clip, part).start()
        return carry

    lax.fori_loop(0, clips * tiles, project, 0)

    strip = 16

    def differentiate(clip):
        for part in range(tiles):
            swap(clip, part).wait()

        def add(step, squares):
            at = pl.ds(multiple(step * strip, strip), strip)
            target = total[clip, at, :] + incoming[clip, at, :].astype(f32)
            total[clip, at, :] = target
            return squares + jnp.sum(target * target, axis=0, keepdims=True)

        squares = lax.fori_loop(0, length // strip, add, jnp.zeros((1, width), f32))
        mean = jnp.sum(squares, axis=1, keepdims=True) / (length * width)
        factor = -2.0 / (jnp.sqrt(mean + 1e-06) + 0.1)

        def scaled(step, carry):
            at = pl.ds(multiple(step * strip, strip), strip)
            cot = total[clip, at, :] * factor
            grad_proj[pl.ds(multiple(clip * length + step * strip, strip), strip), :] = (
                coef[clip, 2:3, :] * cot
            ).astype(half)
            return carry

        lax.fori_loop(0, length // strip, scaled, 0)

    def grad_copies(clip, part):
        result = []
        for slot in range(3):
            at = pl.ds(multiple(part * chunk, 128), chunk)
            out_at = pl.ds(multiple(slot * att + me * att_dev + part * chunk, 128), chunk)
            result.append(
                (
                    pltpu.make_async_remote_copy(
                        src_ref=grads.at[clip, slot, pl.ds(multiple(other * len_dev, 64), len_dev), at],
                        dst_ref=d_qkv.at[clip, :, out_at],
                        send_sem=grad_send.at[clip, part, slot],
                        recv_sem=grad_recv.at[clip, part, slot],
                        device_id={"seq": other},
                        device_id_type=MESH,
                    ),
                    pltpu.make_async_copy(
                        grads.at[clip, slot, pl.ds(multiple(me * len_dev, 64), len_dev), at],
                        d_qkv.at[clip, :, out_at],
                        grad_own.at[clip, part, slot],
                    ),
                )
            )
        return result

    def attend_back(clip, part):
        cosine, sine = cos_tab[clip], sin_tab[clip]
        grad_att = dot(
            grad_proj[pl.ds(multiple(clip * length, length), length), :],
            weight[pl.ds(multiple(part * chunk, 128), chunk), :],
            1,
            1,
        ).astype(half)
        for head in range(chunk // HEAD_DIM):
            at = pl.ds(multiple(part * chunk + head * HEAD_DIM, 128), HEAD_DIM)
            query, key, value = turned[clip, 0, :, at], turned[clip, 1, :, at], turned[clip, 2, :, at]
            upper = grad_att[:, head * HEAD_DIM : (head + 1) * HEAD_DIM]
            probs = softmax_rows(dot(query, key, 1, 1) * scale)
            grad_value = dot(probs.astype(half), upper, 0, 0).astype(half)
            grad_prob = dot(upper, value, 1, 1)
            grad_score = (
                probs * (grad_prob - jnp.sum(probs * grad_prob, axis=-1, keepdims=True)) * scale
            ).astype(half)
            grad_query = dot(grad_score, key, 1, 0).astype(half)
            grad_key = dot(grad_score, query, 0, 0).astype(half)
            grads[clip, 0, :, at] = turn(grad_query, cosine, -sine)
            grads[clip, 1, :, at] = turn(grad_key, cosine, -sine)
            grads[clip, 2, :, at] = grad_value
        for remote, own in grad_copies(clip, part):
            remote.start()
            own.start()

    def back(clip):
        def step(part, carry):
            attend_back(clip, part)
            return carry

        lax.fori_loop(0, chunks, step, 0)

    def block_at(at_plane, at_column, at_core):
        return pl.ds(multiple(index(at_plane, at_column, at_core) * block, 32), block)

    def to_core(step, at_column):
        to_plane = (plane + 1 + step) % PLANES
        return pltpu.make_async_remote_copy(
            src_ref=partial.at[block_at(to_plane, at_column, 1 - core), :],
            dst_ref=from_core.at[step, at_column],
            send_sem=core_send.at[step, at_column],
            recv_sem=core_recv.at[step, at_column],
            device_id={"dp": index(plane, column, 1 - core)},
            device_id_type=MESH,
        )

    def to_column(step):
        to_plane = (plane + 1 + step) % PLANES
        return pltpu.make_async_remote_copy(
            src_ref=partial.at[block_at(to_plane, 1 - column, core), :],
            dst_ref=from_column.at[step],
            send_sem=column_send.at[step],
            recv_sem=column_recv.at[step],
            device_id={"dp": index(plane, 1 - column, core)},
            device_id_type=MESH,
        )

    def to_plane_copy(step):
        to_plane = (plane + 1 + step) % PLANES
        return pltpu.make_async_remote_copy(
            src_ref=partial.at[block_at(to_plane, column, core), :],
            dst_ref=from_plane.at[step],
            send_sem=plane_send.at[step],
            recv_sem=plane_recv.at[step],
            device_id={"dp": index(to_plane, column, core)},
            device_id_type=MESH,
        )

    piece = COLUMNS * CORES * block

    def weight_piece(step, carry):
        to_plane = (plane + 1 + step) % PLANES
        cols = pl.ds(multiple(to_plane * piece, 128), piece)
        left = jnp.concatenate([rows[clip, :length, cols] for clip in range(clips)], 0)

        def one(part, inner):
            at = pl.ds(multiple(part * tile, 128), tile)
            partial[pl.ds(multiple(to_plane * piece, 128), piece), at] = dot(
                left, grad_proj[:, at], 0, 0
            ).astype(half)
            return inner

        lax.fori_loop(0, tiles, one, 0)
        to_core(step, 0).start()
        to_core(step, 1).start()
        return carry

    def add_rows(row, source):
        for lower in range(0, block, 32):
            at = pl.ds(multiple(row * block + lower, 32), 32)
            partial[at, :] = (
                partial[at, :].astype(f32) + source[lower : lower + 32, :].astype(f32)
            ).astype(half)

    def core_stage(step, carry):
        to_plane = (plane + 1 + step) % PLANES
        to_core(step, 0).wait()
        to_core(step, 1).wait()
        for at_column in range(COLUMNS):
            add_rows(index(to_plane, at_column, core), from_core.at[step, at_column])
        to_column(step).start()
        return carry

    def column_stage(step):
        to_plane = (plane + 1 + step) % PLANES
        to_column(step).wait()
        add_rows(index(to_plane, column, core), from_column.at[step])

    def send_plane(step, carry):
        column_stage(step)
        to_plane_copy(step).start()
        return carry

    differentiate(0)
    back(0)
    for clip in range(1, clips):
        differentiate(clip)
    lax.fori_loop(0, PLANES, weight_piece, 0)
    lax.fori_loop(0, PLANES, core_stage, 0)
    for clip in range(1, clips):
        for part in range(chunks):
            attend_back(clip, part)
            if clip == 1:
                send_plane(part, 0)
    column_stage(PLANES - 1)
    for step in range(PLANES - 1):
        to_plane_copy(step).wait()
    root = 1.0 / math.sqrt(token_count)
    for lower in range(0, block, 32):
        own = multiple(index(plane, column, core) * block + lower, 32)
        value = partial[pl.ds(own, 32), :].astype(f32)
        for step in range(PLANES - 1):
            value = value + from_plane[step, lower : lower + 32, :].astype(f32)
        d_weight[lower : lower + 32, :] = value * root

    def finish(step, carry):
        for remote, own in grad_copies(step // chunks, step % chunks):
            remote.wait()
            own.wait()
        return carry

    lax.fori_loop(0, clips * chunks, finish, 0)


def whole_positions(positions, seq_len, len_dev):
    first = (positions[0, :, 0] * GRID_H + positions[1, :, 0]) * GRID_W + positions[2, :, 0]
    first = first - lax.axis_index("seq") * len_dev
    token = first[:, None] + jnp.arange(seq_len, dtype=jnp.int32)[None, :]
    rest = token % (GRID_H * GRID_W)
    return jnp.stack([token // (GRID_H * GRID_W), rest // GRID_W, rest % GRID_W])


def body_pair(
    qkv,
    qkv_tan,
    positions,
    step_index,
    resid,
    resid_tan,
    noisy,
    noisy_tan,
    out_weight,
    gate_bias,
    gate_amp,
    gate_freq,
):
    f32, half = jnp.float32, jnp.bfloat16
    clips, len_dev, triple = qkv.shape
    att_dev = triple // 6
    seq_len = len_dev * 2
    width = resid.shape[2]
    block = out_weight.shape[0]
    angle = rope_angles(whole_positions(positions, seq_len, len_dev))
    angle = jnp.concatenate([angle, angle], -1)
    weight = lax.all_gather(out_weight, "dp", axis=0, tiled=True)
    vmem = pl.BlockSpec(memory_space=pltpu.VMEM)
    hbm = pl.BlockSpec(memory_space=pl.ANY)
    chunks = 3
    dma = pltpu.SemaphoreType.DMA
    rows, turned, cos_tab, sin_tab = pl.pallas_call(
        forward_kernel,
        out_shape=(
            jax.ShapeDtypeStruct((clips, 2 * seq_len, att_dev), half),
            jax.ShapeDtypeStruct((clips, 3, seq_len, att_dev), half),
            jax.ShapeDtypeStruct((clips, seq_len, HEAD_DIM), f32),
            jax.ShapeDtypeStruct((clips, seq_len, HEAD_DIM), f32),
        ),
        in_specs=[hbm, hbm, vmem],
        out_specs=(vmem, vmem, vmem, vmem),
        scratch_shapes=[
            pltpu.VMEM((clips, 6, seq_len, att_dev), half),
            dma((clips, chunks, 6)),
            dma((clips, chunks, 6)),
            dma((clips, chunks, 6)),
        ],
        compiler_params=pltpu.CompilerParams(
            collective_id=0, has_side_effects=True, vmem_limit_bytes=32 * 2**20
        ),
    )(qkv, qkv_tan, angle)

    time = 0.05 + 1.47 * (step_index.astype(f32) + 0.5) / NT
    phase = gate_freq[None, :] * time[:, None]
    gate = gate_bias + gate_amp * jnp.sin(phase)
    slope = gate_amp * gate_freq * jnp.cos(phase)
    cos_sq = (jnp.cos(time) ** 2)[:, None]
    cross = (jnp.cos(time) * jnp.sin(time))[:, None]
    known = -cos_sq[:, :, None] * (0.5 * resid.astype(f32) - noisy_tan.astype(f32)) - cross[
        :, :, None
    ] * (noisy.astype(f32) + 0.5 * resid_tan.astype(f32))
    coef = jnp.stack(
        [-0.5 * (cos_sq * gate + cross * slope), -0.5 * cross * gate, gate], axis=1
    )
    tiles = 5
    return pl.pallas_call(
        backward_kernel,
        out_shape=(
            jax.ShapeDtypeStruct((clips, len_dev, triple), half),
            jax.ShapeDtypeStruct((block, width), f32),
        ),
        in_specs=[vmem] * 7,
        out_specs=(hbm, vmem),
        scratch_shapes=[
            pltpu.VMEM((clips, seq_len, width), f32),
            pltpu.VMEM((clips, seq_len, width), half),
            pltpu.VMEM((clips, seq_len, width), half),
            pltpu.VMEM((clips * seq_len, width), half),
            pltpu.VMEM((clips, 3, seq_len, att_dev), half),
            pltpu.VMEM((att_dev, width), half),
            pltpu.VMEM((PLANES, COLUMNS, block, width), half),
            pltpu.VMEM((PLANES, block, width), half),
            pltpu.VMEM((PLANES - 1, block, width), half),
            dma((clips, tiles)),
            dma((clips, tiles)),
            dma((clips, chunks, 3)),
            dma((clips, chunks, 3)),
            dma((clips, chunks, 3)),
            dma((PLANES, COLUMNS)),
            dma((PLANES, COLUMNS)),
            dma((PLANES,)),
            dma((PLANES,)),
            dma((PLANES - 1,)),
            dma((PLANES - 1,)),
        ],
        compiler_params=pltpu.CompilerParams(
            collective_id=1, has_side_effects=True, vmem_limit_bytes=58 * 2**20
        ),
    )(weight, rows, turned, known, coef, cos_tab, sin_tab)


def solution(mesh):
    placed = (
        P("dp", "seq", None),
        P("dp", "seq", None),
        P(None, "dp", "seq"),
        P("dp"),
        P("dp", "seq", None),
        P("dp", "seq", None),
        P("dp", "seq", None),
        P("dp", "seq", None),
        P(("seq", "dp"), None),
        P(),
        P(),
        P(),
    )
    fits = mesh.shape["dp"] == PLANES * COLUMNS * CORES and mesh.shape["seq"] == 2
    return jax.shard_map(
        body_pair if fits else body,
        mesh=mesh,
        in_specs=placed,
        out_specs=(P("dp", "seq", None), P(("seq", "dp"), None)),
        check_vma=False,
    )
```

profile of v0, /device:TPU:9, one launch (start us, length us, event | category | flops | bytes accessed | tf_op | source)
XLA Modules:
  0.0 195.1 jit_solution(4003302425972970753)
XLA Ops:
  7.2 0.0 all-gather.2.cloned.1.call-start
  7.2 0.7 all-gather.2.cloned.1.call-update
  7.9 0.7 mul.216
  8.7 0.8 subtract_reduce_fusion
  9.5 0.1 and_select_fusion.3
  9.6 0.2 select_multiply_fusion
  9.8 0.1 pad_maximum_fusion.angle
  9.9 1.7 copy-done.1
  11.6 1.7 copy-done.2
  13.2 0.0 copy-start.7
  13.3 0.0 copy-start.8
  13.3 55.3 %shard_map.131 = (bf16[2,256,1536]{2,1,0:T(8,128)(2,1)S(1)}, bf16[2,3,128,1536]{3,2,1,0:T(8,128)(2,1)S(1)}, f32[2,128,128]{2,1,0:T(8,128)S(1)}, f32[2,128,128]{2,1,0:T(8,128)S(1)}) custom-call(bf16[2,64,9216]{2,1,0:T(8,128)(2,1)S(1)} %copy-done.1, bf16[2,64,9216]{2,1,0:T(8,128)(2,1)S(1)} %copy-done.2, f32[2,128,128]{2,1,0:T(8,128)S(1)} %pad_maximum_fusion.angle), custom_call_target="tpu_custom_call" | custom-call | tf_op jit(solution)/shard_map/pallas_call | solution.py:622
  68.6 1.4 copy-done
  70.0 1.1 copy-done.3
  71.2 0.7 copy-done.4
  71.8 0.7 copy-done.5
  72.6 0.7 fusion.5
  73.3 0.1 broadcast_multiply_fusion
  73.4 0.7 pad_maximum_fusion.1.coef
  74.1 1.6 multiply_subtract_fusion.known
  75.7 7.4 %all-gather.2.cloned.1.call-done.weight = bf16[1536,2560]{1,0:T(8,128)(2,1)} async-done(((bf16[96,2560]{1,0:T(8,128)(2,1)}), bf16[1536,2560]{1,0:T(8,128)(2,1)}) %all-gather.2.cloned.1.call-update) | async-done | bytes 7864336 | tf_op jit(solution)/shard_map/all_gather | solution.py:617
  83.1 100.9 %shard_map.132 = (bf16[2,64,9216]{2,1,0:T(8,128)(2,1)}, f32[96,2560]{1,0:T(8,128)}) custom-call(bf16[1536,2560]{1,0:T(8,128)(2,1)} %all-gather.2.cloned.1.call-done.weight, bf16[2,256,1536]{2,1,0:T(8,128)(2,1)} %copy-done.3, bf16[2,3,128,1536]{3,2,1,0:T(8,128)(2,1)} %copy-done, f32[2,64,2560]{2,1,0:T(8,128)} %multiply_subtract_fusion.known, ...), custom_call_target="tpu_custom_call" | custom-call | tf_op jit(solution)/shard_map/pallas_call | solution.py:656
  184.0 3.3 %copy.18 = bf16[2,64,9216]{2,1,0:T(8,128)(2,1)} copy(bf16[2,64,9216]{2,1,0:T(8,128)(2,1)} %get-tuple-element.29) | data formatting | bytes 4718592
  187.3 0.9 copy.19
  (27 shorter events, 0.1 us)
Async XLA Ops:
  7.2 75.9 %all-gather.2.cloned.1.call-start = ((), (), s32[]{:S(2)}) async-start(), calls=%async_computation | async-start | bytes 8355840 | tf_op jit(solution)/shard_map/all_gather | solution.py:617
  9.9 1.7 copy-start.1
  11.6 1.7 copy-start.2
  13.2 59.3 %copy-start.14 = (s32[2]{0:T(128)S(1)}, s32[2]{0:T(128)}, u32[]{:S(2)}) copy-start(s32[2]{0:T(128)} %param.15) | copy-start | bytes 28
  13.2 59.3 %copy-start.11 = (f32[2560]{0:T(1024)S(1)}, f32[2560]{0:T(1024)}, u32[]{:S(2)}) copy-start(f32[2560]{0:T(1024)} %param.22) | copy-start | bytes 30724
  13.2 59.3 %copy-start.12 = (f32[2560]{0:T(1024)S(1)}, f32[2560]{0:T(1024)}, u32[]{:S(2)}) copy-start(f32[2560]{0:T(1024)} %param.23) | copy-start | bytes 30724
  13.2 59.3 %copy-start.13 = (f32[2560]{0:T(1024)S(1)}, f32[2560]{0:T(1024)}, u32[]{:S(2)}) copy-start(f32[2560]{0:T(1024)} %param.21) | copy-start | bytes 30724
  13.2 60.8 %copy-start.7 = (bf16[2,64,2560]{2,1,0:T(8,128)(2,1)S(1)}, bf16[2,64,2560]{2,1,0:T(8,128)(2,1)}, u32[]{:S(2)}) copy-start(bf16[2,64,2560]{2,1,0:T(8,128)(2,1)} %param.17) | copy-start | bytes 1966084
  13.3 60.8 %copy-start.8 = (bf16[2,64,2560]{2,1,0:T(8,128)(2,1)S(1)}, bf16[2,64,2560]{2,1,0:T(8,128)(2,1)}, u32[]{:S(2)}) copy-start(bf16[2,64,2560]{2,1,0:T(8,128)(2,1)} %param.18) | copy-start | bytes 1966084
  13.3 60.8 %copy-start.9 = (bf16[2,64,2560]{2,1,0:T(8,128)(2,1)S(1)}, bf16[2,64,2560]{2,1,0:T(8,128)(2,1)}, u32[]{:S(2)}) copy-start(bf16[2,64,2560]{2,1,0:T(8,128)(2,1)} %param.19) | copy-start | bytes 1966084
  13.3 60.8 %copy-start.10 = (bf16[2,64,2560]{2,1,0:T(8,128)(2,1)S(1)}, bf16[2,64,2560]{2,1,0:T(8,128)(2,1)}, u32[]{:S(2)}) copy-start(bf16[2,64,2560]{2,1,0:T(8,128)(2,1)} %param.16) | copy-start | bytes 1966084
  68.6 1.4 copy-start
  70.0 1.1 copy-start.3
  71.2 0.7 copy-start.4
  71.8 0.7 copy-start.5
  184.0 3.3 %copy-start.6 = (f32[96,2560]{1,0:T(8,128)S(1)}, f32[96,2560]{1,0:T(8,128)}, u32[]{:S(2)}) copy-start(f32[96,2560]{1,0:T(8,128)} %get-tuple-element.30) | copy-start | bytes 2949124
Sparse Core Ops, SparseCore 0:
  10.3 72.7 all-gather.1
where the time goes:
time: 196 us; the launch traced here: 195 us
  Pallas kernels  156 us (80%)
  between operations  14.2 us (7%)
  local copies, waits for them, and re-layouts  11.5 us (6%)
  waiting for transfers between devices  8.06 us (4%)
  other arithmetic  5.08 us (3%)
    pallas_call x1, Pallas kernels, body_pair(): pl.pallas_call(backward_kernel, out_shape=(jax.ShapeDtypeStruct((clips, l...  101 us
    pallas_call x1, Pallas kernels, body_pair(): pl.pallas_call(forward_kernel, out_shape=(jax.ShapeDtypeStruct((clips, 2...  55.3 us
    unnamed x32, local copies, waits for them, and re-layouts  11.5 us
    all_gather x1, waiting for transfers between devices, body_pair(): weight = lax.all_gather(out_weight, 'dp', axis=0, tiled=True)  7.38 us
  transfers between devices with their start and end apart: 1, of which 1 were waited for; matrix products, arithmetic and copies ran while one was open for 3% of the time, Pallas kernels for 28%

commit v1 on v0

--- a/solution.py
+++ b/solution.py
@@ -209,21 +209,116 @@
     return (wide * cosine + pltpu.roll(wide, HEAD_DIM // 2, 1) * sine).astype(jnp.bfloat16)
 
 
-def forward_kernel(
-    qkv, qkv_tan, angle, rows, turned, cos_out, sin_out, arrived, send_sem, recv_sem, own_sem
+def step_kernel(
+    qkv,
+    qkv_tan,
+    angle,
+    own_weight,
+    known,
+    coef,
+    d_qkv,
+    d_weight,
+    arrived,
+    rows,
+    cos_tab,
+    sin_tab,
+    weight,
+    total,
+    outgoing,
+    incoming,
+    grad_proj,
+    grads,
+    partial,
+    from_core,
+    from_column,
+    from_plane,
+    send_sem,
+    recv_sem,
+    own_sem,
+    spread_send,
+    spread_recv,
+    swap_send,
+    swap_recv,
+    grad_send,
+    grad_recv,
+    grad_own,
+    core_send,
+    core_recv,
+    column_send,
+    column_recv,
+    plane_send,
+    plane_recv,
 ):
+    f32, half = jnp.float32, jnp.bfloat16
     me = lax.axis_index("seq")
     other = 1 - me
-    clips, len_dev, triple = qkv.shape
-    att = triple // 3
-    att_dev = att // 2
-    chunks = send_sem.shape[1]
+    place = lax.axis_index("dp")
+    plane, column, core = place // (COLUMNS * CORES), (place // CORES) % COLUMNS, place % CORES
+
+    def index(at_plane, at_column, at_core):
+        return (at_plane * COLUMNS + at_column) * CORES + at_core
+
+    clips, length, width = total.shape
+    att_dev = weight.shape[0]
+    len_dev = length // 2
+    att = att_dev * 2
+    scale = 1.0 / math.sqrt(HEAD_DIM)
+    block = d_weight.shape[0]
+    tiles = swap_send.shape[1]
+    tile = width // tiles
+    chunks = grad_send.shape[1]
     chunk = att_dev // chunks
-    scale = 1.0 / math.sqrt(HEAD_DIM)
+    token_count = lax.axis_size("dp") * clips * length
 
     barrier = pltpu.get_barrier_semaphore()
     pl.semaphore_signal(barrier, inc=1, device_id={"seq": other}, device_id_type=MESH)
-    pl.semaphore_wait(barrier, 1)
+    partners = [index(plane, column, 1 - core), index(plane, 1 - column, core)]
+    partners += [index((plane + 1 + step) % PLANES, column, core) for step in range(PLANES - 1)]
+    for partner in partners:
+        pl.semaphore_signal(barrier, inc=1, device_id={"dp": partner}, device_id_type=MESH)
+    pl.semaphore_wait(barrier, 1 + len(partners))
+
+    def block_at(at_plane, at_column, at_core):
+        return pl.ds(multiple(index(at_plane, at_column, at_core) * block, 32), block)
+
+    def spread(at_plane, at_column, slot, partner, own=False):
+        there = block_at(at_plane, at_column, core)
+        return pltpu.make_async_remote_copy(
+            src_ref=own_weight if own else weight.at[there, :],
+            dst_ref=weight.at[there, :],
+            send_sem=spread_send.at[slot],
+            recv_sem=spread_recv.at[slot],
+            device_id={"dp": partner},
+            device_id_type=MESH,
+        )
+
+    sibling, beside = index(plane, column, 1 - core), index(plane, 1 - column, core)
+
+    def to_planes(step):
+        return spread(
+            plane, column, step, index((plane + 1 + step) % PLANES, column, core), own=True
+        )
+
+    def behind(step):
+        return (plane + PLANES - step) % PLANES
+
+    def to_beside(step):
+        return spread(behind(step), column, PLANES - 1 + step, beside, own=step == 0)
+
+    def to_sibling(step, swapped):
+        at_column = 1 - column if swapped else column
+        return spread(
+            behind(step),
+            at_column,
+            2 * PLANES - 1 + 2 * step + swapped,
+            sibling,
+            own=step == 0 and not swapped,
+        )
+
+    for step in range(PLANES - 1):
+        to_planes(step).start()
+    to_beside(0).start()
+    to_sibling(0, 0).start()
 
     def copies(clip, part):
         result = []
@@ -263,17 +358,18 @@
         return carry
 
     lax.fori_loop(0, clips * chunks, start, 0)
+    weight[block_at(plane, column, core), :] = own_weight[...]
     lane = lax.broadcasted_iota(jnp.int32, angle.shape, 2)
     sines = jnp.sin(angle[...])
-    cos_out[...] = jnp.cos(angle[...])
-    sin_out[...] = jnp.where(lane < HEAD_DIM // 2, -sines, sines)
+    cos_tab[...] = jnp.cos(angle[...])
+    sin_tab[...] = jnp.where(lane < HEAD_DIM // 2, -sines, sines)
 
     def attend(step, carry):
         clip, part = step // chunks, step % chunks
         for remote, own in copies(clip, part):
             remote.wait()
             own.wait()
-        cosine, sine = cos_out[clip], sin_out[clip]
+        cosine, sine = cos_tab[clip], sin_tab[clip]
         for head in range(chunk // HEAD_DIM):
             at = pl.ds(multiple(part * chunk + head * HEAD_DIM, 128), HEAD_DIM)
             query = turn(arrived[clip, 0, :, at], cosine, sine)
@@ -282,85 +378,49 @@
             query_tan = turn(arrived[clip, 3, :, at], cosine, sine)
             key_tan = turn(arrived[clip, 4, :, at], cosine, sine)
             value_tan = arrived[clip, 5, :, at]
-            turned[clip, 0, :, at] = query
-            turned[clip, 1, :, at] = key
-            turned[clip, 2, :, at] = value
+            arrived[clip, 0, :, at] = query
+            arrived[clip, 1, :, at] = key
             probs = softmax_rows(dot(query, key, 1, 1) * scale)
-            low = probs.astype(jnp.bfloat16)
-            length = low.shape[0]
-            rows[clip, :length, at] = dot(low, value, 1, 0).astype(jnp.bfloat16)
+            low = probs.astype(half)
+            rows[clip, :length, at] = dot(low, value, 1, 0).astype(half)
             dscore = scale * dot(
                 jnp.concatenate([query_tan, query], 1), jnp.concatenate([key, key_tan], 1), 1, 1
             )
             dprob = probs * (dscore - jnp.sum(probs * dscore, axis=-1, keepdims=True))
-            both = jnp.concatenate([dprob.astype(jnp.bfloat16), low], 1)
+            both = jnp.concatenate([dprob.astype(half), low], 1)
             rows[clip, length:, at] = dot(
                 both, jnp.concatenate([value, value_tan], 0), 1, 0
-            ).astype(jnp.bfloat16)
+            ).astype(half)
         return carry
 
-    lax.fori_loop(0, clips * chunks, attend, 0)
-
-
-def backward_kernel(
-    weight,
-    rows,
-    turned,
-    known,
-    coef,
-    cos_tab,
-    sin_tab,
-    d_qkv,
-    d_weight,
-    total,
-    outgoing,
-    incoming,
-    grad_proj,
-    grads,
-    partial,
-    from_core,
-    from_column,
-    from_plane,
-    swap_send,
-    swap_recv,
-    grad_send,
-    grad_recv,
-    grad_own,
-    core_send,
-    core_recv,
-    column_send,
-    column_recv,
-    plane_send,
-    plane_recv,
-):
-    f32, half = jnp.float32, jnp.bfloat16
-    me = lax.axis_index("seq")
-    other = 1 - me
-    place = lax.axis_index("dp")
-    plane, column, core = place // (COLUMNS * CORES), (place // CORES) % COLUMNS, place % CORES
-
-    def index(at_plane, at_column, at_core):
-        return (at_plane * COLUMNS + at_column) * CORES + at_core
-
-    clips, length, width = total.shape
-    att_dev = weight.shape[0]
-    len_dev = length // 2
-    att = att_dev * 2
-    scale = 1.0 / math.sqrt(HEAD_DIM)
-    block = d_weight.shape[0]
-    tiles = swap_send.shape[1]
-    tile = width // tiles
-    chunks = grad_send.shape[1]
-    chunk = att_dev // chunks
-    token_count = lax.axis_size("dp") * clips * length
-
-    barrier = pltpu.get_barrier_semaphore()
-    pl.semaphore_signal(barrier, inc=1, device_id={"seq": other}, device_id_type=MESH)
-    partners = [index(plane, column, 1 - core), index(plane, 1 - column, core)]
-    partners += [index((plane + 1 + step) % PLANES, column, core) for step in range(PLANES - 1)]
-    for partner in partners:
-        pl.semaphore_signal(barrier, inc=1, device_id={"dp": partner}, device_id_type=MESH)
-    pl.semaphore_wait(barrier, 1 + len(partners))
+    lax.fori_loop(0, 2, attend, 0)
+    to_planes(0).wait_recv()
+    to_beside(1).start()
+    to_sibling(1, 0).start()
+    to_beside(0).wait_recv()
+    to_sibling(0, 1).start()
+    lax.fori_loop(2, 3, attend, 0)
+    to_planes(1).wait_recv()
+    to_beside(2).start()
+    to_sibling(2, 0).start()
+    lax.fori_loop(3, 4, attend, 0)
+    to_planes(2).wait_recv()
+    to_beside(3).start()
+    to_sibling(3, 0).start()
+    to_beside(1).wait_recv()
+    to_sibling(1, 1).start()
+    lax.fori_loop(4, 5, attend, 0)
+    to_beside(2).wait_recv()
+    to_sibling(2, 1).start()
+    lax.fori_loop(5, clips * chunks, attend, 0)
+    to_beside(3).wait_recv()
+    to_sibling(3, 1).start()
+    for step in range(PLANES - 1):
+        to_planes(step).wait_send()
+    for step in range(PLANES):
+        to_beside(step).wait_send()
+        to_sibling(step, 0).wait()
+        to_sibling(step, 1).wait()
 
     def swap(clip, part):
         at = pl.ds(multiple(part * tile, 128), tile)
@@ -448,7 +508,7 @@
         ).astype(half)
         for head in range(chunk // HEAD_DIM):
             at = pl.ds(multiple(part * chunk + head * HEAD_DIM, 128), HEAD_DIM)
-            query, key, value = turned[clip, 0, :, at], turned[clip, 1, :, at], turned[clip, 2, :, at]
+            query, key, value = arrived[clip, 0, :, at], arrived[clip, 1, :, at], arrived[clip, 2, :, at]
             upper = grad_att[:, head * HEAD_DIM : (head + 1) * HEAD_DIM]
             probs = softmax_rows(dot(query, key, 1, 1) * scale)
             grad_value = dot(probs.astype(half), upper, 0, 0).astype(half)
@@ -471,9 +531,6 @@
             return carry
 
         lax.fori_loop(0, chunks, step, 0)
-
-    def block_at(at_plane, at_column, at_core):
-        return pl.ds(multiple(index(at_plane, at_column, at_core) * block, 32), block)
 
     def to_core(step, at_column):
         to_plane = (plane + 1 + step) % PLANES
@@ -614,32 +671,10 @@
     block = out_weight.shape[0]
     angle = rope_angles(whole_positions(positions, seq_len, len_dev))
     angle = jnp.concatenate([angle, angle], -1)
-    weight = lax.all_gather(out_weight, "dp", axis=0, tiled=True)
     vmem = pl.BlockSpec(memory_space=pltpu.VMEM)
     hbm = pl.BlockSpec(memory_space=pl.ANY)
     chunks = 3
     dma = pltpu.SemaphoreType.DMA
-    rows, turned, cos_tab, sin_tab = pl.pallas_call(
-        forward_kernel,
-        out_shape=(
-            jax.ShapeDtypeStruct((clips, 2 * seq_len, att_dev), half),
-            jax.ShapeDtypeStruct((clips, 3, seq_len, att_dev), half),
-            jax.ShapeDtypeStruct((clips, seq_len, HEAD_DIM), f32),
-            jax.ShapeDtypeStruct((clips, seq_len, HEAD_DIM), f32),
-        ),
-        in_specs=[hbm, hbm, vmem],
-        out_specs=(vmem, vmem, vmem, vmem),
-        scratch_shapes=[
-            pltpu.VMEM((clips, 6, seq_len, att_dev), half),
-            dma((clips, chunks, 6)),
-            dma((clips, chunks, 6)),
-            dma((clips, chunks, 6)),
-        ],
-        compiler_params=pltpu.CompilerParams(
-            collective_id=0, has_side_effects=True, vmem_limit_bytes=32 * 2**20
-        ),
-    )(qkv, qkv_tan, angle)
-
     time = 0.05 + 1.47 * (step_index.astype(f32) + 0.5) / NT
     phase = gate_freq[None, :] * time[:, None]
     gate = gate_bias + gate_amp * jnp.sin(phase)
@@ -654,14 +689,19 @@
     )
     tiles = 5
     return pl.pallas_call(
-        backward_kernel,
+        step_kernel,
         out_shape=(
             jax.ShapeDtypeStruct((clips, len_dev, triple), half),
             jax.ShapeDtypeStruct((block, width), f32),
         ),
-        in_specs=[vmem] * 7,
+        in_specs=[hbm, hbm, vmem, vmem, vmem, vmem],
         out_specs=(hbm, vmem),
         scratch_shapes=[
+            pltpu.VMEM((clips, 6, seq_len, att_dev), half),
+            pltpu.VMEM((clips, 2 * seq_len, att_dev), half),
+            pltpu.VMEM((clips, seq_len, HEAD_DIM), f32),
+            pltpu.VMEM((clips, seq_len, HEAD_DIM), f32),
+            pltpu.VMEM((att_dev, width), half),
             pltpu.VMEM((clips, seq_len, width), f32),
             pltpu.VMEM((clips, seq_len, width), half),
             pltpu.VMEM((clips, seq_len, width), half),
@@ -671,6 +711,11 @@
             pltpu.VMEM((PLANES, COLUMNS, block, width), half),
             pltpu.VMEM((PLANES, block, width), half),
             pltpu.VMEM((PLANES - 1, block, width), half),
+            dma((clips, chunks, 6)),
+            dma((clips, chunks, 6)),
+            dma((clips, chunks, 6)),
+            dma((4 * PLANES - 1,)),
+            dma((4 * PLANES - 1,)),
             dma((clips, tiles)),
             dma((clips, tiles)),
             dma((clips, chunks, 3)),
@@ -684,9 +729,9 @@
             dma((PLANES - 1,)),
         ],
         compiler_params=pltpu.CompilerParams(
-            collective_id=1, has_side_effects=True, vmem_limit_bytes=58 * 2**20
+            collective_id=0, has_side_effects=True, vmem_limit_bytes=58 * 2**20
         ),
-    )(weight, rows, turned, known, coef, cos_tab, sin_tab)
+    )(qkv, qkv_tan, angle, out_weight, known, coef)
 
 
 def solution(mesh):

time: 196 us -> 183 us (0.934)
  between operations: 14.2 us -> 0.7 us
  Pallas kernels: 156 us -> 169 us
  waiting for transfers between devices: 8.06 us -> 0 us
  local copies, waits for them, and re-layouts: 11.5 us -> 4.26 us
  other arithmetic: 5.08 us -> 8.73 us
    pallas_call x2 -> x1, Pallas kernels: 156 us -> 169 us  [body_pair(): pl.pallas_call(step_kernel, out_shape=(jax.ShapeDtypeStruct((clips, len_d...]
    all_gather x1 -> x0, waiting for transfers between devices: 7.38 us -> none  [body_pair(): weight = lax.all_gather(out_weight, 'dp', axis=0, tiled=True)]
    unnamed x32 -> x4, local copies, waits for them, and re-layouts: 11.5 us -> 4.25 us
  transfers between devices with their start and end apart: 1 -> 0, of which waited for: 1 -> 0; matrix products, arithmetic and copies ran while one was open for 3% -> 0% of each run, Pallas kernels for 28% -> 0%
where the time goes in v1:
time: 183 us
  Pallas kernels  169 us (92%)
  other arithmetic  8.73 us (5%)
  local copies, waits for them, and re-layouts  4.26 us (2%)
    pallas_call x1, Pallas kernels, body_pair(): pl.pallas_call(step_kernel, out_shape=(jax.ShapeDtypeStruct((clips, len_d...  169 us
    unnamed x4, local copies, waits for them, and re-layouts  4.25 us

profile of v1, /device:TPU:9, one launch (start us, length us, event | category | flops | bytes accessed | tf_op | source)
XLA Modules:
  0.0 183.0 jit_solution(8319878768595735694)
XLA Ops:
  0.6 0.8 subtract_reduce_fusion
  1.5 0.7 multiply_add_fusion
  2.2 0.1 and_select_fusion.3
  2.3 0.7 mul.216
  3.1 1.4 fusion.5
  4.5 0.1 broadcast_multiply_fusion
  4.6 0.7 pad_maximum_fusion.1.coef
  5.3 0.2 select_multiply_fusion
  5.4 0.8 pad_maximum_fusion.angle
  6.2 3.2 %multiply_subtract_fusion.known = f32[2,64,2560]{2,1,0:T(8,128)} fusion(bf16[2,64,2560]{2,1,0:T(8,128)(2,1)} %param.17, bf16[2,64,2560]{2,1,0:T(8,128)(2,1)} %param.18, bf16[2,64,2560]{2,1,0:T(8,128)(2,1)} %param.19, bf16[2,64,2560]{2,1,0:T(8,128)(2,1)} %param.16, f32[2]{0:T(128)S(1)} %get-tuple-element.13, f32[2]{0:T(128)S(1)} %get-tuple-element.10), kind=kLoop, calls=%fused_computation | loop fusion | flops 3604480 | bytes 3932176 | tf_op jit(solution)/shard_map/sub | solution.py:684
  9.4 169.3 %shard_map.131 = (bf16[2,64,9216]{2,1,0:T(8,128)(2,1)}, f32[96,2560]{1,0:T(8,128)}) custom-call(bf16[2,64,9216]{2,1,0:T(8,128)(2,1)} %qkv.1, bf16[2,64,9216]{2,1,0:T(8,128)(2,1)} %qkv_tan.1, f32[2,128,128]{2,1,0:T(8,128)} %pad_maximum_fusion.angle, bf16[96,2560]{1,0:T(8,128)(2,1)} %own_weight.1, f32[2,64,2560]{2,1,0:T(8,128)} %multiply_subtract_fusion.known, ...), custom_call_target="tpu_custom_call" | custom-call | tf_op jit(solution)/shard_map/pallas_call | solution.py:691
  178.7 0.0 copy-start
  178.7 3.3 %copy.18 = bf16[2,64,9216]{2,1,0:T(8,128)(2,1)} copy(bf16[2,64,9216]{2,1,0:T(8,128)(2,1)} %get-tuple-element.21) | data formatting | bytes 4718592
  182.0 0.0 copy-done
  182.0 0.9 copy.19
  (4 shorter events, 0.0 us)
Async XLA Ops:
  178.7 3.3 %copy-start = (f32[96,2560]{1,0:T(8,128)S(1)}, f32[96,2560]{1,0:T(8,128)}, u32[]{:S(2)}) copy-start(f32[96,2560]{1,0:T(8,128)} %get-tuple-element.22) | copy-start | bytes 2949124
